TPU v7x, 32 devices: a whole 2x2x4 slice. The times are simulated.
32 devices in a mesh: group: 2 (over y), row: 2 (over core), col: 8 (over z, x).
Axes of the slice: x: 2, y: 2, z: 4, core: 2. Of those that a mesh axis runs over, the one named last changes fastest.
Arguments:
- tokens: bfloat16 [1024, 8192], P(('group', 'col'), 'row'), parts along dimension 0, may hold values from -6 to 6
- cotangent: bfloat16 [1024, 8192], P(('group', 'col'), 'row'), parts along dimension 0, may hold values from -6 to 6
- gate_weight: bfloat16 [8192, 16384], P('row', 'col'), may hold values from -0.09375 to 0.09375
- up_weight: bfloat16 [8192, 16384], P('row', 'col'), may hold values from -0.09375 to 0.09375
- down_weight: bfloat16 [16384, 8192], P('col', 'row'), may hold values from -0.0625 to 0.0625
- gate_mask: int32 [64, 128], P('row', 'col'), may hold values from 0 to 1, as said below
- up_mask: int32 [64, 128], P('row', 'col'), may hold values from 0 to 1, as said below
- down_mask: int32 [128, 64], P('col', 'row'), may hold values from 0 to 1, as said below
Outputs:
- output: bfloat16 [1024, 8192], P(('group', 'col'), 'row'), parts along dimension 0
- input_grad: bfloat16 [1024, 8192], P(('group', 'col'), 'row'), parts along dimension 0
- gate_grad: bfloat16 [16384, 16384], P(('group', 'row'), 'col'), parts along dimension 0
- up_grad: bfloat16 [16384, 16384], P(('group', 'row'), 'col'), parts along dimension 0
- down_grad: bfloat16 [32768, 8192], P(('group', 'col'), 'row'), parts along dimension 0
There are 2 independent parts, one for each index of `group`. A program takes and returns all parts, laid end to end along the dimension named above; an argument that names none is the same for every part. Nothing has to cross between parts.
Inputs may be any that keep to these rules, and one draw needn't show every extreme that they name: `gate_mask`: 1 keeps a 128 x 128 block of the projection, 0 removes it. `up_mask`: 1 keeps a 128 x 128 block of the projection, 0 removes it. `down_mask`: 1 keeps a 128 x 128 block of the projection, 0 removes it.
All inputs are finite; a program needn't handle non-finite values.
Results may differ from a plain program's by a relative error of at most 0.005.
Values may be sent and summed in bfloat16 or wider, within the bound.
A program may use at most 320 MiB of HBM per device.

v0:
```python
import jax
import jax.numpy as jnp
from jax import lax
from jax.sharding import PartitionSpec as P

BLOCK = 128


def spread(block_mask):
    row_blocks, col_blocks = block_mask.shape
    expanded = jnp.broadcast_to(
        block_mask.astype(jnp.bfloat16)[:, None, :, None], (row_blocks, BLOCK, col_blocks, BLOCK)
    )
    return expanded.reshape(row_blocks * BLOCK, col_blocks * BLOCK)


def contract_rows(left, right):
    return lax.dot_general(
        left, right, (((0,), (0,)), ((), ())), preferred_element_type=jnp.float32
    )


def body(tokens, cotangent, gate_weight, up_weight, down_weight, gate_mask, up_mask, down_mask):
    gate_keep = spread(gate_mask)
    up_keep = spread(up_mask)
    down_keep = spread(down_mask)
    both_eff = jnp.concatenate([gate_weight * gate_keep, up_weight * up_keep], axis=1)
    down_eff = down_weight * down_keep
    hidden_cols = gate_weight.shape[1]
    gathered = lax.all_gather(tokens, "col", axis=0, tiled=True)
    partial_sums = lax.psum(jnp.dot(gathered, both_eff, preferred_element_type=jnp.float32), "row")
    gate_pre = partial_sums[:, :hidden_cols]
    up_pre = partial_sums[:, hidden_cols:]
    sigmoid_gate = jax.nn.sigmoid(gate_pre)
    activated = gate_pre * sigmoid_gate
    hidden = (activated * up_pre).astype(jnp.bfloat16)
    row_block = hidden
    output = lax.psum_scatter(
        jnp.dot(row_block, down_eff, preferred_element_type=jnp.float32),
        "col",
        scatter_dimension=0,
        tiled=True,
    ).astype(jnp.bfloat16)
    shard_rows = lax.all_gather(cotangent, "col", axis=0, tiled=True)
    term = lax.dot_general(
        shard_rows, down_eff, (((1,), (1,)), ((), ())), preferred_element_type=jnp.float32
    )
    row_block = hidden
    down_total = contract_rows(row_block, shard_rows)
    hidden_grad = lax.psum(term, "row")
    gate_delta = (
        hidden_grad * up_pre * sigmoid_gate * (1.0 + gate_pre * (1.0 - sigmoid_gate))
    ).astype(jnp.bfloat16)
    up_delta = (hidden_grad * activated).astype(jnp.bfloat16)
    both_delta = jnp.concatenate([gate_delta, up_delta], axis=1)
    row_block = both_delta
    input_grad = lax.psum_scatter(
        lax.dot_general(
            row_block, both_eff, (((1,), (1,)), ((), ())), preferred_element_type=jnp.float32
        ),
        "col",
        scatter_dimension=0,
        tiled=True,
    ).astype(jnp.bfloat16)
    features = lax.all_gather(tokens, "col", axis=0, tiled=True)
    gate_grad = (contract_rows(features, gate_delta) * gate_keep).astype(jnp.bfloat16)
    up_grad = (contract_rows(features, up_delta) * up_keep).astype(jnp.bfloat16)
    down_grad = (down_total * down_keep).astype(jnp.bfloat16)
    return (output, input_grad, gate_grad, up_grad, down_grad)


def solution(mesh):
    in_specs = (
        P(("group", "col"), "row"),
        P(("group", "col"), "row"),
        P("row", "col"),
        P("row", "col"),
        P("col", "row"),
        P("row", "col"),
        P("row", "col"),
        P("col", "row"),
    )
    out_specs = (
        P(("group", "col"), "row"),
        P(("group", "col"), "row"),
        P(("group", "row"), "col"),
        P(("group", "row"), "col"),
        P(("group", "col"), "row"),
    )
    return jax.shard_map(body, mesh=mesh, in_specs=in_specs, out_specs=out_specs, check_vma=False)
```

profile of v0, /device:TPU:0, one launch (start us, length us, event | category | flops | bytes accessed | tf_op | source)
XLA Modules:
  0.0 578.8 jit_solution(12022222742906459888)
XLA Ops:
  8.7 0.7 convert_element_type.42
  10.8 21.2 %copy.13 = bf16[4096,2048]{0,1:T(8,128)(2,1)} copy(bf16[4096,2048]{1,0:T(8,128)(2,1)} %param.10) | data formatting | bytes 33554432 | tf_op args[2]
  32.0 21.4 %copy.14 = bf16[4096,2048]{0,1:T(8,128)(2,1)} copy(bf16[4096,2048]{1,0:T(8,128)(2,1)} %param.11) | data formatting | bytes 33554432 | tf_op args[3]
  53.5 6.2 %broadcast_in_dim.7 = bf16[32,128,16,128]{1,0,3,2:T(8,128)(2,1)} broadcast(bf16[32,16]{0,1:T(8,128)(2,1)S(1)} %convert_element_type.43), dimensions={0,2} | broadcast | bytes 16778240 | tf_op jit(solution)/shard_map/broadcast_in_dim | solution.py:11
  59.7 2.8 broadcast_in_dim.6
  62.5 5.7 copy-done
  68.2 30.1 %bitcast_multiply_fusion.3 = (bf16[4096,2048]{0,1:T(8,128)(2,1)}, bf16[4096,2048]{0,1:T(8,128)(2,1)}) fusion(bf16[4096,2048]{0,1:T(8,128)(2,1)} %copy.14, bf16[256,8,32,128]{3,2,1,0:T(8,128)(2,1)} %bitcast.46, bf16[4096,2048]{0,1:T(8,128)(2,1)} %copy.13, bf16[256,8,32,128]{3,2,1,0:T(8,128)(2,1)S(1)} %bitcast.44), kind=kLoop, calls=%fused_computation.9 | loop fusion | flops 16777216 | bytes 100663296 | tf_op jit(solution)/shard_map/mul | solution.py:27
  98.3 6.3 %broadcast_in_dim.8 = bf16[16,128,32,128]{3,2,1,0:T(8,128)(2,1)} broadcast(bf16[16,32]{1,0:T(8,128)(2,1)S(1)} %convert_element_type.45), dimensions={0,2} | broadcast | bytes 16778240 | tf_op jit(solution)/shard_map/broadcast_in_dim | solution.py:11
  104.6 19.3 %fusion.11 = f32[512,2048]{0,1:T(8,128)} fusion(bf16[512,4096]{1,0:T(8,128)(2,1)} %all-gather.5.cloned.1.call-done, bf16[2048,4096]{1,0:T(8,128)(2,1)} %param.12, bf16[256,8,32,128]{3,2,1,0:T(8,128)(2,1)} %bitcast.48), kind=kOutput, calls=%fused_computation.22 | convolution fusion | flops 8598323200 | bytes 41943040 | tf_op jit(solution)/shard_map/dot_general | solution.py:45
  123.9 36.2 %all-gather.3.cloned.1.call-done = bf16[512,4096]{1,0:T(8,128)(2,1)} async-done(((bf16[64,4096]{1,0:T(8,128)(2,1)}), bf16[512,4096]{1,0:T(8,128)(2,1)}) %all-gather.3.cloned.1.call-update) | async-done | bytes 4194320 | tf_op jit(solution)/shard_map/all_gather | solution.py:30
  160.1 24.8 %fusion.4 = f32[512,4096]{0,1:T(8,128)} fusion(bf16[512,4096]{1,0:T(8,128)(2,1)} %all-gather.3.cloned.1.call-done, bf16[4096,2048]{0,1:T(8,128)(2,1)} %get-tuple-element.15, bf16[4096,2048]{0,1:T(8,128)(2,1)} %get-tuple-element.16), kind=kOutput, calls=%fused_computation.11 | convolution fusion | flops 17246978048 | bytes 46137344 | tf_op jit(solution)/shard_map/dot_general | solution.py:31
  185.0 47.9 %all-reduce.3.cloned.1.call-done = (f32[512,4096]{0,1:T(8,128)}, f32[512,2048]{0,1:T(8,128)}) async-done(((f32[512,4096]{0,1:T(8,128)}, f32[512,2048]{0,1:T(8,128)}), (f32[512,4096]{0,1:T(8,128)}, f32[512,2048]{0,1:T(8,128)})) %all-reduce.3.cloned.1.call-update) | async-done | bytes 12582928 | tf_op jit(solution)/shard_map/psum | solution.py:31
  232.8 7.4 %multiply_convert_fusion.2 = (bf16[512,2048]{0,1:T(8,128)(2,1)}, bf16[512,2048]{0,1:T(8,128)(2,1)}, bf16[512,2048]{0,1:T(8,128)(2,1)S(1)}) fusion(f32[512,2048]{0,1:T(8,128)} %get-tuple-element.11, f32[512,4096]{0,1:T(8,128)} %get-tuple-element.10), kind=kLoop, calls=%fused_computation.18 | loop fusion | flops 15728640 | bytes 18874368 | tf_op jit(solution)/shard_map/convert_element_type | solution.py:53
  240.3 27.4 %fusion.2 = f32[512,4096]{1,0:T(8,128)} fusion(bf16[4096,2048]{0,1:T(8,128)(2,1)} %get-tuple-element.15, bf16[4096,2048]{0,1:T(8,128)(2,1)} %get-tuple-element.16, bf16[512,2048]{0,1:T(8,128)(2,1)} %get-tuple-element.13, bf16[512,2048]{0,1:T(8,128)(2,1)} %get-tuple-element.12), kind=kOutput, calls=%fused_computation.6 | convolution fusion | flops 17255366656 | bytes 46137344 | tf_op jit(solution)/shard_map/dot_general | solution.py:58
  267.8 18.2 %fusion.6 = f32[512,4096]{1,0:T(8,128)} fusion(bf16[512,2048]{0,1:T(8,128)(2,1)S(1)} %get-tuple-element.14, bf16[2048,4096]{1,0:T(8,128)(2,1)} %param.12, bf16[256,8,32,128]{3,2,1,0:T(8,128)(2,1)} %bitcast.49), kind=kOutput, calls=%fused_computation.13 | convolution fusion | flops 8598323200 | bytes 44040192 | tf_op jit(solution)/shard_map/dot_general | solution.py:39
  285.9 19.2 %fusion = bf16[4096,2048]{0,1:T(8,128)(2,1)} fusion(bf16[512,2048]{0,1:T(8,128)(2,1)} %get-tuple-element.13, bf16[512,4096]{1,0:T(8,128)(2,1)} %all-gather.3.cloned.1.call-done, bf16[256,8,32,128]{3,2,1,0:T(8,128)(2,1)} %bitcast.47), kind=kOutput, calls=%fused_computation.2 | convolution fusion | flops 8615100416 | bytes 39845888 | tf_op jit(solution)/shard_map/dot_general | solution.py:18
  305.2 22.5 %copy.16 = bf16[4096,2048]{1,0:T(8,128)(2,1)} copy(bf16[4096,2048]{0,1:T(8,128)(2,1)} %fusion) | data formatting | bytes 33554432
  327.7 19.5 %fusion.1 = bf16[4096,2048]{0,1:T(8,128)(2,1)} fusion(bf16[512,2048]{0,1:T(8,128)(2,1)} %get-tuple-element.12, bf16[512,4096]{1,0:T(8,128)(2,1)} %all-gather.3.cloned.1.call-done, bf16[256,8,32,128]{3,2,1,0:T(8,128)(2,1)} %bitcast.45), kind=kOutput, calls=%fused_computation.4 | convolution fusion | flops 8615100416 | bytes 39845888 | tf_op jit(solution)/shard_map/dot_general | solution.py:18
  347.2 22.5 %copy.15 = bf16[4096,2048]{1,0:T(8,128)(2,1)} copy(bf16[4096,2048]{0,1:T(8,128)(2,1)} %fusion.1) | data formatting | bytes 33554432
  369.7 18.6 %multiply_convert_fusion = bf16[2048,4096]{1,0:T(8,128)(2,1)} fusion(bf16[512,2048]{0,1:T(8,128)(2,1)S(1)} %get-tuple-element.14, bf16[512,4096]{1,0:T(8,128)(2,1)} %all-gather.5.cloned.1.call-done, bf16[256,8,32,128]{3,2,1,0:T(8,128)(2,1)} %bitcast.50), kind=kOutput, calls=%fused_computation.5 | convolution fusion | flops 8615100416 | bytes 39845888 | tf_op jit(solution)/shard_map/dot_general | solution.py:18
  388.4 29.6 %reduce-scatter.5.cloned.1.call-done = f32[64,4096]{1,0:T(8,128)} async-done(((f32[512,4096]{1,0:T(8,128)}), f32[64,4096]{1,0:T(8,128)}) %reduce-scatter.5.cloned.1.call-update) | async-done | bytes 1048592 | tf_op jit(solution)/shard_map/reduce_scatter | solution.py:57
  417.9 2.1 convert_element_type.49
  420.0 150.0 %reduce-scatter.3.cloned.1.call-done = f32[64,4096]{1,0:T(8,128)} async-done(((f32[512,4096]{1,0:T(8,128)}), f32[64,4096]{1,0:T(8,128)}) %reduce-scatter.3.cloned.1.call-update) | async-done | bytes 1048592 | tf_op jit(solution)/shard_map/reduce_scatter | solution.py:38
  570.0 2.1 convert_element_type.46
  (14 shorter events, 3.0 us)
Async XLA Ops:
  7.2 91.2 %all-gather.5.cloned.1.call-start = ((), (), s32[]{:S(2)}) async-start(), calls=%async_computation.4 | async-start | bytes 4718592 | tf_op jit(solution)/shard_map/all_gather | solution.py:44
  7.9 152.2 %all-gather.3.cloned.1.call-start = ((), (), s32[]{:S(2)}) async-start(), calls=%async_computation.2 | async-start | bytes 4718592 | tf_op jit(solution)/shard_map/all_gather | solution.py:30
  8.6 224.2 %all-reduce.3.cloned.1.call-start = ((), (), s32[]{:S(2)}) async-start(), calls=%async_computation.6 | async-start | bytes 25165824 | tf_op jit(solution)/shard_map/psum | solution.py:31
  62.5 5.7 copy-start
  184.9 233.0 %reduce-scatter.5.cloned.1.call-start = ((), (), s32[]{:S(2)}) async-start(), calls=%async_computation.5 | async-start | bytes 9437184 | tf_op jit(solution)/shard_map/reduce_scatter | solution.py:57
  267.7 302.3 %reduce-scatter.3.cloned.1.call-start = ((), (), s32[]{:S(2)}) async-start(), calls=%async_computation.3 | async-start | bytes 9437184 | tf_op jit(solution)/shard_map/reduce_scatter | solution.py:38
Sparse Core Ops, SparseCore 0:
  10.1 76.0 all-gather.4
  88.4 71.6 all-gather.2
  185.0 47.7 all-reduce.2
  267.8 150.0 reduce-scatter.4
  421.9 148.0 reduce-scatter.2
where the time goes:
time: 588 us; the launch traced here: 579 us
  waiting for transfers between devices  265 us (45%)
  matrix products  147 us (25%)
  local copies, waits for them, and re-layouts  109 us (19%)
  other arithmetic  43.8 us (7%)
  between operations  14 us (2%)
    reduce_scatter x1, waiting for transfers between devices, body(): lax.psum_scatter(jnp.dot(row_block, down_eff, preferred_element_type=jnp....  150 us
    unnamed x6, local copies, waits for them, and re-layouts  93.4 us
    dot_general x3, matrix products, contract_rows(): lax.dot_general(left, right, (((0,), (0,)), ((), ())), preferred_element_...  57.4 us
    psum x1, waiting for transfers between devices, body(): lax.psum(jnp.dot(gathered, both_eff, preferred_element_type=jnp.float32),...  47.9 us
    all_gather x1, waiting for transfers between devices, body(): gathered = lax.all_gather(tokens, 'col', axis=0, tiled=True)  36.2 us
    mul x1, other arithmetic, body(): up_weight * up_keep  30.1 us
    reduce_scatter x1, waiting for transfers between devices, body(): lax.psum_scatter(lax.dot_general(row_block, both_eff, (((1,), (1,)), ((),...  29.6 us
    dot_general x1, matrix products, body(): lax.dot_general(row_block, both_eff, (((1,), (1,)), ((), ())), preferred_...  27.4 us
  transfers between devices with their start and end apart: 5, of which 4 were waited for; matrix products, arithmetic and copies ran while one was open for 40% of the time, Pallas kernels for 0%

commit v1 on v0

--- a/solution.py
+++ b/solution.py
@@ -4,6 +4,27 @@
 from jax.sharding import PartitionSpec as P
 
 BLOCK = 128
+
+
+def gather_around(x, axis, dim):
+    size, index, span = (lax.axis_size(axis), lax.axis_index(axis), x.shape[dim])
+    right = [(i, (i + 1) % size) for i in range(size)]
+    left = [(i, (i - 1) % size) for i in range(size)]
+    filled = jnp.zeros((*x.shape[:dim], size * span, *x.shape[dim + 1 :]), x.dtype)
+    filled = lax.dynamic_update_slice_in_dim(filled, x, index * span, axis=dim)
+    from_left = from_right = x
+    half = size // 2
+    for step in range(1, half + 1):
+        from_left = lax.ppermute(from_left, axis, right)
+        filled = lax.dynamic_update_slice_in_dim(
+            filled, from_left, (index - step) % size * span, axis=dim
+        )
+        if step < size - half:
+            from_right = lax.ppermute(from_right, axis, left)
+            filled = lax.dynamic_update_slice_in_dim(
+                filled, from_right, (index + step) % size * span, axis=dim
+            )
+    return filled
 
 
 def spread(block_mask):
@@ -27,7 +48,7 @@
     both_eff = jnp.concatenate([gate_weight * gate_keep, up_weight * up_keep], axis=1)
     down_eff = down_weight * down_keep
     hidden_cols = gate_weight.shape[1]
-    gathered = lax.all_gather(tokens, "col", axis=0, tiled=True)
+    gathered = gather_around(tokens, "col", 0)
     partial_sums = lax.psum(jnp.dot(gathered, both_eff, preferred_element_type=jnp.float32), "row")
     gate_pre = partial_sums[:, :hidden_cols]
     up_pre = partial_sums[:, hidden_cols:]

time: 588 us -> 661 us (1.12)
  waiting for transfers between devices: 265 us -> 296 us
  starting transfers between devices: 0.2 us -> 28.9 us
  matrix products: 147 us -> 158 us
  local copies, waits for them, and re-layouts: 109 us -> 117 us
    reduce_scatter x1, waiting for transfers between devices: 29.6 us -> 150 us  [body(): lax.psum_scatter(lax.dot_general(row_block, both_eff, (((1,), (1,)), ((),...]
    reduce_scatter x1, waiting for transfers between devices: 150 us -> 38.1 us  [body(): lax.psum_scatter(jnp.dot(row_block, down_eff, preferred_element_type=jnp....]
    ppermute x0 -> x7, waiting for transfers between devices: none -> 35 us  [the longest x4 34.9 us: gather_around(): from_left = lax.ppermute(from_left, axis, right)]
    ppermute x0 -> x7, starting transfers between devices: none -> 28.5 us  [the longest x3 20.1 us: gather_around(): from_right = lax.ppermute(from_right, axis, left)]
    all_gather x1, waiting for transfers between devices: 36.2 us -> 24.2 us  [body(): features = lax.all_gather(tokens, 'col', axis=0, tiled=True)]
    dot_general x3, matrix products: 57.4 us -> 67.7 us  [contract_rows(): lax.dot_general(left, right, (((0,), (0,)), ((), ())), preferred_element_...]
    dynamic_update_slice x0 -> x8, local copies, waits for them, and re-layouts: none -> 6.66 us  [the longest x4 3.32 us: gather_around(): lax.dynamic_update_slice_in_dim(filled, from_left, (index - step) % size...]
    unnamed x6 -> x14, local copies, waits for them, and re-layouts: 93.4 us -> 91.1 us
  transfers between devices with their start and end apart: 5 -> 12, of which waited for: 4 -> 7; matrix products, arithmetic and copies ran while one was open for 40% -> 43% of each run, Pallas kernels for 0% -> 0%
where the time goes in v1:
time: 661 us; the launch traced here: 655 us
  waiting for transfers between devices  296 us (45%)
  matrix products  158 us (24%)
  local copies, waits for them, and re-layouts  117 us (18%)
  other arithmetic  41.8 us (6%)
  starting transfers between devices  28.9 us (4%)
  between operations  14.1 us (2%)
    reduce_scatter x1, waiting for transfers between devices, body(): lax.psum_scatter(lax.dot_general(row_block, both_eff, (((1,), (1,)), ((),...  150 us
    unnamed x14, local copies, waits for them, and re-layouts  91.1 us
    dot_general x3, matrix products, contract_rows(): lax.dot_general(left, right, (((0,), (0,)), ((), ())), preferred_element_...  67.7 us
    psum x1, waiting for transfers between devices, body(): lax.psum(jnp.dot(gathered, both_eff, preferred_element_type=jnp.float32),...  47.7 us
    reduce_scatter x1, waiting for transfers between devices, body(): lax.psum_scatter(jnp.dot(row_block, down_eff, preferred_element_type=jnp....  38.1 us
    ppermute x4, waiting for transfers between devices, gather_around(): from_left = lax.ppermute(from_left, axis, right)  34.9 us
    mul x1, other arithmetic, body(): up_weight * up_keep  30.1 us
    dot_general x1, matrix products, body(): lax.dot_general(row_block, both_eff, (((1,), (1,)), ((), ())), preferred_...  27.1 us
  transfers between devices with their start and end apart: 12, of which 7 were waited for; matrix products, arithmetic and copies ran while one was open for 43% of the time, Pallas kernels for 0%

profile of v1, /device:TPU:0, one launch (start us, length us, event | category | flops | bytes accessed | tf_op | source)
XLA Modules:
  0.0 654.7 jit_solution(147431393244426089)
XLA Ops:
  13.4 21.3 %copy.14 = bf16[4096,2048]{0,1:T(8,128)(2,1)} copy(bf16[4096,2048]{1,0:T(8,128)(2,1)} %param.11) | data formatting | bytes 33554432 | tf_op args[3]
  34.7 21.4 %copy.13 = bf16[4096,2048]{0,1:T(8,128)(2,1)} copy(bf16[4096,2048]{1,0:T(8,128)(2,1)} %param.10) | data formatting | bytes 33554432 | tf_op args[2]
  59.0 7.4 %broadcast_in_dim.9 = bf16[32,128,16,128]{1,0,3,2:T(8,128)(2,1)} broadcast(bf16[32,16]{0,1:T(8,128)(2,1)S(1)} %convert_element_type.42), dimensions={0,2} | broadcast | bytes 16778240 | tf_op jit(solution)/shard_map/broadcast_in_dim | solution.py:32
  69.7 30.1 %bitcast_multiply_fusion.3 = (bf16[4096,2048]{0,1:T(8,128)(2,1)}, bf16[4096,2048]{0,1:T(8,128)(2,1)}) fusion(bf16[4096,2048]{0,1:T(8,128)(2,1)} %copy.14, bf16[256,8,32,128]{3,2,1,0:T(8,128)(2,1)S(1)} %bitcast.42, bf16[4096,2048]{0,1:T(8,128)(2,1)} %copy.13, bf16[256,8,32,128]{3,2,1,0:T(8,128)(2,1)} %bitcast.44), kind=kLoop, calls=%fused_computation.9 | loop fusion | flops 16777216 | bytes 100663296 | tf_op jit(solution)/shard_map/mul | solution.py:48
  103.2 4.7 collective-permute-start.3
  109.5 16.0 %collective-permute-done.2 = bf16[64,4096]{1,0:T(8,128)(2,1)S(1)} collective-permute-done((bf16[64,4096]{1,0:T(8,128)(2,1)S(1)}, bf16[64,4096]{1,0:T(8,128)(2,1)S(1)}, u32[]{:S(2)}, u32[]{:S(2)}) %collective-permute-start.2) | collective-permute-done | bytes 524320 | tf_op jit(solution)/shard_map/ppermute | solution.py:18
  128.0 12.2 %collective-permute-start.5 = (bf16[64,4096]{1,0:T(8,128)(2,1)S(1)}, bf16[64,4096]{1,0:T(8,128)(2,1)S(1)}, u32[]{:S(2)}, u32[]{:S(2)}) collective-permute-start(bf16[64,4096]{1,0:T(8,128)(2,1)S(1)} %collective-permute-done.3), channel_id=1, source_target_pairs={{0,7},{1,0},{2,1},{3,2},{4,3},{5,4},{6,5},{7,6},{8,15},{9,8},{10,9... | collective-permute-start | bytes 1572872 | tf_op jit(solution)/shard_map/ppermute | solution.py:23
  141.9 7.6 %collective-permute-done.4 = bf16[64,4096]{1,0:T(8,128)(2,1)S(1)} collective-permute-done((bf16[64,4096]{1,0:T(8,128)(2,1)S(1)}, bf16[64,4096]{1,0:T(8,128)(2,1)S(1)}, u32[]{:S(2)}, u32[]{:S(2)}) %collective-permute-start.4) | collective-permute-done | bytes 524320 | tf_op jit(solution)/shard_map/ppermute | solution.py:18
  154.1 11.4 %collective-permute-done.6 = bf16[64,4096]{1,0:T(8,128)(2,1)S(1)} collective-permute-done((bf16[64,4096]{1,0:T(8,128)(2,1)S(1)}, bf16[64,4096]{1,0:T(8,128)(2,1)S(1)}, u32[]{:S(2)}, u32[]{:S(2)}) %collective-permute-start.6) | collective-permute-done | bytes 524320 | tf_op jit(solution)/shard_map/ppermute | solution.py:18
  166.4 25.4 %fusion.3 = f32[512,4096]{1,0:T(8,128)} fusion(bf16[512,4096]{1,0:T(8,128)(2,1)} %constant_dynamic-update-slice_fusion, bf16[4096,2048]{0,1:T(8,128)(2,1)} %get-tuple-element.15, bf16[4096,2048]{0,1:T(8,128)(2,1)} %get-tuple-element.16), kind=kOutput, calls=%fused_computation.7 | convolution fusion | flops 17246978048 | bytes 46137344 | tf_op jit(solution)/shard_map/dot_general | solution.py:52
  191.7 6.2 broadcast_in_dim.11
  197.9 19.7 %fusion.10 = f32[512,2048]{1,0:T(8,128)} fusion(bf16[512,4096]{1,0:T(8,128)(2,1)} %all-gather.3.cloned.1.call-done, bf16[2048,4096]{1,0:T(8,128)(2,1)} %param.12, bf16[256,8,32,128]{3,2,1,0:T(8,128)(2,1)} %bitcast.46), kind=kOutput, calls=%fused_computation.21 | convolution fusion | flops 8598323200 | bytes 41943040 | tf_op jit(solution)/shard_map/dot_general | solution.py:66
  218.6 47.7 %all-reduce.3.cloned.1.call-done = (f32[512,4096]{1,0:T(8,128)}, f32[512,2048]{1,0:T(8,128)}) async-done(((f32[512,4096]{1,0:T(8,128)}, f32[512,2048]{1,0:T(8,128)}), (f32[512,4096]{1,0:T(8,128)}, f32[512,2048]{1,0:T(8,128)})) %all-reduce.3.cloned.1.call-update) | async-done | bytes 12582928 | tf_op jit(solution)/shard_map/psum | solution.py:52
  266.3 7.6 %multiply_convert_fusion.2 = (bf16[512,2048]{1,0:T(8,128)(2,1)}, bf16[512,2048]{1,0:T(8,128)(2,1)}, bf16[512,2048]{1,0:T(8,128)(2,1)S(1)}) fusion(f32[512,2048]{1,0:T(8,128)} %get-tuple-element.11, f32[512,4096]{1,0:T(8,128)} %get-tuple-element.10), kind=kLoop, calls=%fused_computation.17 | loop fusion | flops 15728640 | bytes 18874368 | tf_op jit(solution)/shard_map/convert_element_type | solution.py:74
  273.9 17.7 %fusion.5 = f32[512,4096]{1,0:T(8,128)} fusion(bf16[512,2048]{1,0:T(8,128)(2,1)S(1)} %get-tuple-element.14, bf16[2048,4096]{1,0:T(8,128)(2,1)} %param.12, bf16[256,8,32,128]{3,2,1,0:T(8,128)(2,1)} %bitcast.47), kind=kOutput, calls=%fused_computation.12 | convolution fusion | flops 8598323200 | bytes 44040192 | tf_op jit(solution)/shard_map/dot_general | solution.py:60
  291.7 27.1 %fusion.2 = f32[512,4096]{1,0:T(8,128)} fusion(bf16[4096,2048]{0,1:T(8,128)(2,1)} %get-tuple-element.15, bf16[4096,2048]{0,1:T(8,128)(2,1)} %get-tuple-element.16, bf16[512,2048]{1,0:T(8,128)(2,1)} %get-tuple-element.13, bf16[512,2048]{1,0:T(8,128)(2,1)} %get-tuple-element.12), kind=kOutput, calls=%fused_computation.6 | convolution fusion | flops 17255366656 | bytes 46137344 | tf_op jit(solution)/shard_map/dot_general | solution.py:79
  318.9 24.2 %all-gather.5.cloned.1.call-done = bf16[512,4096]{1,0:T(8,128)(2,1)} async-done(((bf16[64,4096]{1,0:T(8,128)(2,1)}), bf16[512,4096]{1,0:T(8,128)(2,1)}) %all-gather.5.cloned.1.call-update) | async-done | bytes 4194320 | tf_op jit(solution)/shard_map/all_gather | solution.py:86
  343.1 22.4 %fusion.1 = bf16[4096,2048]{0,1:T(8,128)(2,1)} fusion(bf16[512,2048]{1,0:T(8,128)(2,1)} %get-tuple-element.12, bf16[512,4096]{1,0:T(8,128)(2,1)} %all-gather.5.cloned.1.call-done, bf16[256,8,32,128]{3,2,1,0:T(8,128)(2,1)} %bitcast.45), kind=kOutput, calls=%fused_computation.4 | convolution fusion | flops 8615100416 | bytes 39845888 | tf_op jit(solution)/shard_map/dot_general | solution.py:39
  365.5 22.5 %copy.16 = bf16[4096,2048]{1,0:T(8,128)(2,1)} copy(bf16[4096,2048]{0,1:T(8,128)(2,1)} %fusion.1) | data formatting | bytes 33554432
  388.0 22.9 %fusion = bf16[4096,2048]{0,1:T(8,128)(2,1)} fusion(bf16[512,2048]{1,0:T(8,128)(2,1)} %get-tuple-element.13, bf16[512,4096]{1,0:T(8,128)(2,1)} %all-gather.5.cloned.1.call-done, bf16[256,8,32,128]{3,2,1,0:T(8,128)(2,1)} %bitcast.43), kind=kOutput, calls=%fused_computation.2 | convolution fusion | flops 8615100416 | bytes 39845888 | tf_op jit(solution)/shard_map/dot_general | solution.py:39
  410.9 22.5 %copy.17 = bf16[4096,2048]{1,0:T(8,128)(2,1)} copy(bf16[4096,2048]{0,1:T(8,128)(2,1)} %fusion) | data formatting | bytes 33554432
  433.4 22.5 %multiply_convert_fusion = bf16[2048,4096]{1,0:T(8,128)(2,1)} fusion(bf16[512,2048]{1,0:T(8,128)(2,1)S(1)} %get-tuple-element.14, bf16[512,4096]{1,0:T(8,128)(2,1)} %all-gather.3.cloned.1.call-done, bf16[256,8,32,128]{3,2,1,0:T(8,128)(2,1)} %bitcast.48), kind=kOutput, calls=%fused_computation.5 | convolution fusion | flops 8615100416 | bytes 39845888 | tf_op jit(solution)/shard_map/dot_general | solution.py:39
  455.8 38.1 %reduce-scatter.3.cloned.1.call-done = f32[64,4096]{1,0:T(8,128)} async-done(((f32[512,4096]{1,0:T(8,128)}), f32[64,4096]{1,0:T(8,128)}) %reduce-scatter.3.cloned.1.call-update) | async-done | bytes 1048592 | tf_op jit(solution)/shard_map/reduce_scatter | solution.py:59
  496.0 149.9 %reduce-scatter.5.cloned.1.call-done = f32[64,4096]{1,0:T(8,128)} async-done(((f32[512,4096]{1,0:T(8,128)}), f32[64,4096]{1,0:T(8,128)}) %reduce-scatter.5.cloned.1.call-update) | async-done | bytes 1048592 | tf_op jit(solution)/shard_map/reduce_scatter | solution.py:78
  (45 shorter events, 32.1 us)
Async XLA Ops:
  7.2 184.6 %all-gather.3.cloned.1.call-start = ((), (), s32[]{:S(2)}) async-start(), calls=%async_computation.3 | async-start | bytes 4718592 | tf_op jit(solution)/shard_map/all_gather | solution.py:65
  7.2 95.9 %collective-permute-start = (bf16[64,4096]{1,0:T(8,128)(2,1)}, bf16[64,4096]{1,0:T(8,128)(2,1)S(1)}, u32[]{:S(2)}, u32[]{:S(2)}) collective-permute-start(bf16[64,4096]{1,0:T(8,128)(2,1)} %param.8), channel_id=1, source_target_pairs={{0,1},{1,2},{2,3},{3,4},{4,5},{5,6},{6,7},{7,0},{8,9},{9,10},{10,1... | collective-permute-start | bytes 1572872 | tf_op jit(solution)/shard_map/ppermute | solution.py:18
  10.2 93.0 %collective-permute-start.1 = (bf16[64,4096]{1,0:T(8,128)(2,1)}, bf16[64,4096]{1,0:T(8,128)(2,1)S(1)}, u32[]{:S(2)}, u32[]{:S(2)}) collective-permute-start(bf16[64,4096]{1,0:T(8,128)(2,1)} %param.8), channel_id=1, source_target_pairs={{0,7},{1,0},{2,1},{3,2},{4,3},{5,4},{6,5},{7,6},{8,15},{9,8},{10,9... | collective-permute-start | bytes 1572872 | tf_op jit(solution)/shard_map/ppermute | solution.py:23
  13.3 21.3 %copy-start.2 = (s32[32,16]{0,1:T(8,128)S(1)}, s32[32,16]{0,1:T(8,128)}, u32[]{:S(2)}) copy-start(s32[32,16]{0,1:T(8,128)} %param.14) | copy-start | bytes 6148
  13.3 253.0 %all-reduce.3.cloned.1.call-start = ((), (), s32[]{:S(2)}) async-start(), calls=%async_computation.6 | async-start | bytes 25165824 | tf_op jit(solution)/shard_map/psum | solution.py:52
  34.7 21.4 %copy-start.3 = (s32[32,16]{0,1:T(8,128)S(1)}, s32[32,16]{0,1:T(8,128)}, u32[]{:S(2)}) copy-start(s32[32,16]{0,1:T(8,128)} %param.13) | copy-start | bytes 6148
  59.0 10.8 %copy-start = (bf16[32,128,16,128]{1,0,3,2:T(8,128)(2,1)}, bf16[32,128,16,128]{1,0,3,2:T(8,128)(2,1)S(1)}, u32[]{:S(2)}) copy-start(bf16[32,128,16,128]{1,0,3,2:T(8,128)(2,1)S(1)} %broadcast_in_dim.10) | copy-start | bytes 50331652
  69.7 30.1 %copy-start.4 = (s32[16,32]{1,0:T(8,128)S(1)}, s32[16,32]{1,0:T(8,128)}, u32[]{:S(2)}) copy-start(s32[16,32]{1,0:T(8,128)} %param.15) | copy-start | bytes 6148
  69.7 32.6 %copy-start.1 = (bf16[64,4096]{1,0:T(8,128)(2,1)S(1)}, bf16[64,4096]{1,0:T(8,128)(2,1)}, u32[]{:S(2)}) copy-start(bf16[64,4096]{1,0:T(8,128)(2,1)} %param.8) | copy-start | bytes 1572868
  103.2 22.4 %collective-permute-start.2 = (bf16[64,4096]{1,0:T(8,128)(2,1)S(1)}, bf16[64,4096]{1,0:T(8,128)(2,1)S(1)}, u32[]{:S(2)}, u32[]{:S(2)}) collective-permute-start(bf16[64,4096]{1,0:T(8,128)(2,1)S(1)} %collective-permute-done), channel_id=1, source_target_pairs={{0,1},{1,2},{2,3},{3,4},{4,5},{5,6},{6,7},{7,0},{8,9},{9,10},{10,1... | collective-permute-start | bytes 1572872 | tf_op jit(solution)/shard_map/ppermute | solution.py:18
  103.2 24.8 %collective-permute-start.3 = (bf16[64,4096]{1,0:T(8,128)(2,1)S(1)}, bf16[64,4096]{1,0:T(8,128)(2,1)S(1)}, u32[]{:S(2)}, u32[]{:S(2)}) collective-permute-start(bf16[64,4096]{1,0:T(8,128)(2,1)S(1)} %collective-permute-done.1), channel_id=1, source_target_pairs={{0,7},{1,0},{2,1},{3,2},{4,3},{5,4},{6,5},{7,6},{8,15},{9,8},{10,9... | collective-permute-start | bytes 1572872 | tf_op jit(solution)/shard_map/ppermute | solution.py:23
  125.5 24.0 %collective-permute-start.4 = (bf16[64,4096]{1,0:T(8,128)(2,1)S(1)}, bf16[64,4096]{1,0:T(8,128)(2,1)S(1)}, u32[]{:S(2)}, u32[]{:S(2)}) collective-permute-start(bf16[64,4096]{1,0:T(8,128)(2,1)S(1)} %collective-permute-done.2), channel_id=1, source_target_pairs={{0,1},{1,2},{2,3},{3,4},{4,5},{5,6},{6,7},{7,0},{8,9},{9,10},{10,1... | collective-permute-start | bytes 1572872 | tf_op jit(solution)/shard_map/ppermute | solution.py:18
  128.0 25.3 %collective-permute-start.5 = (bf16[64,4096]{1,0:T(8,128)(2,1)S(1)}, bf16[64,4096]{1,0:T(8,128)(2,1)S(1)}, u32[]{:S(2)}, u32[]{:S(2)}) collective-permute-start(bf16[64,4096]{1,0:T(8,128)(2,1)S(1)} %collective-permute-done.3), channel_id=1, source_target_pairs={{0,7},{1,0},{2,1},{3,2},{4,3},{5,4},{6,5},{7,6},{8,15},{9,8},{10,9... | collective-permute-start | bytes 1572872 | tf_op jit(solution)/shard_map/ppermute | solution.py:23
  149.5 16.1 %collective-permute-start.6 = (bf16[64,4096]{1,0:T(8,128)(2,1)S(1)}, bf16[64,4096]{1,0:T(8,128)(2,1)S(1)}, u32[]{:S(2)}, u32[]{:S(2)}) collective-permute-start(bf16[64,4096]{1,0:T(8,128)(2,1)S(1)} %collective-permute-done.4), channel_id=1, source_target_pairs={{0,1},{1,2},{2,3},{3,4},{4,5},{5,6},{6,7},{7,0},{8,9},{9,10},{10,1... | collective-permute-start | bytes 1572872 | tf_op jit(solution)/shard_map/ppermute | solution.py:18
  217.6 125.4 %all-gather.5.cloned.1.call-start = ((), (), s32[]{:S(2)}) async-start(), calls=%async_computation.5 | async-start | bytes 4718592 | tf_op jit(solution)/shard_map/all_gather | solution.py:86
  218.4 275.5 %reduce-scatter.3.cloned.1.call-start = ((), (), s32[]{:S(2)}) async-start(), calls=%async_computation.2 | async-start | bytes 9437184 | tf_op jit(solution)/shard_map/reduce_scatter | solution.py:59
  291.7 354.2 %reduce-scatter.5.cloned.1.call-start = ((), (), s32[]{:S(2)}) async-start(), calls=%async_computation.4 | async-start | bytes 9437184 | tf_op jit(solution)/shard_map/reduce_scatter | solution.py:78
Sparse Core Ops, SparseCore 0:
  13.5 78.9 all-gather.2
  217.8 48.5 all-reduce.2
  268.5 74.5 all-gather.4
  346.5 147.3 reduce-scatter.2
  497.8 148.0 reduce-scatter.4
